TPU v7x, 128 devices: a whole 4x4x4 slice. The times are simulated.
128 devices in a mesh: gx: 2 (over core), gy: 16 (over y, x), gz: 4 (over z).
Axes of the slice: x: 4, y: 4, z: 4, core: 2. Of those that a mesh axis runs over, the one named last changes fastest.
Arguments:
- field: float32 [512, 512, 1024], P('gx', 'gy', 'gz'), may hold values from -60 to 60
- start_one: float32 [512, 128], replicated, may hold values from -6 to 6
- start_two: float32 [512, 128], replicated, may hold values from -6 to 6
Outputs:
- basis_one: float32 [512, 128], P('gx')
- basis_two: float32 [512, 128], P('gy')
- core: float32 [128, 128, 1024], P('gx', 'gy', 'gz')
All inputs are finite; a program needn't handle non-finite values.
Results may differ from a plain program's by a relative error of at most 0.00024.
Values sent between devices are 32-bit elements; how exact they have to be, the bound alone decides.
A program may use at most 128 MiB of HBM per device.

v0:
```python
import jax
import jax.numpy as jnp
from jax import lax
from jax.sharding import PartitionSpec as P

RANK = 128
ITERS = 2


highest = lax.Precision.HIGHEST


def cholesky_step(product, crossed):
    factor = jnp.linalg.cholesky(crossed)
    return jax.scipy.linalg.solve_triangular(factor, product.T, lower=True).T


def orthonormal_split(row_block, start_basis, total_fn, spread_fn):
    current = start_basis
    local_rows = start_basis
    for step in range(ITERS):
        product = jnp.dot(row_block, current, precision=highest)
        crossed = total_fn(jnp.dot(product.T, product, precision=highest))
        local_rows = cholesky_step(product, crossed)
        if step + 1 < ITERS:
            current = spread_fn(local_rows)
    return local_rows


def body(field, start_one, start_two):
    rows_one, cols_two, depth = field.shape
    ranks_one = RANK // lax.axis_size("gx")
    ranks_two = RANK // lax.axis_size("gy")
    own_flat = field.reshape(rows_one, -1)
    kept_one = lax.all_gather(field, "gx", axis=0, tiled=True)
    kept_flat = kept_one.reshape(kept_one.shape[0], -1)
    gram_rows = jnp.dot(own_flat, kept_flat.T, precision=highest)
    gram_rows = lax.psum(gram_rows, ("gy", "gz"))
    local_one = orthonormal_split(
        gram_rows,
        start_one,
        lambda value: lax.psum(value, "gx"),
        lambda value: lax.all_gather(value, "gx", axis=0, tiled=True),
    )
    whole_one = lax.all_gather(local_one, "gx", axis=0, tiled=True)
    own_cols = lax.dynamic_slice_in_dim(whole_one, lax.axis_index("gx") * ranks_one, ranks_one, 1)
    projected = jnp.dot(own_cols.T, kept_flat, precision=highest).reshape(
        ranks_one, cols_two, depth
    )
    kept_two = lax.all_gather(projected, "gy", axis=1, tiled=True)
    gram_rows_two = lax.dot_general(
        projected, kept_two, (((0, 2), (0, 2)), ((), ())), precision=highest
    )
    gram_rows_two = lax.psum(gram_rows_two, ("gx", "gz"))
    local_two = orthonormal_split(
        gram_rows_two,
        start_two,
        lambda value: lax.psum(value, "gy"),
        lambda value: lax.all_gather(value, "gy", axis=0, tiled=True),
    )
    whole_two = lax.all_gather(local_two, "gy", axis=0, tiled=True)
    own_cols_two = lax.dynamic_slice_in_dim(
        whole_two, lax.axis_index("gy") * ranks_two, ranks_two, 1
    )
    core_rows = lax.dot_general(own_cols_two, kept_two, (((0,), (1,)), ((), ())), precision=highest)
    core = jnp.transpose(core_rows, (1, 0, 2))
    return (local_one, local_two, core)


def solution(mesh):
    return jax.shard_map(
        body,
        mesh=mesh,
        in_specs=(P("gx", "gy", "gz"), P(), P()),
        out_specs=(P("gx", None), P("gy", None), P("gx", "gy", "gz")),
        check_vma=False,
    )
```

profile of v0, /device:TPU:1, one launch (start us, length us, event | category | flops | bytes accessed | tf_op | source)
XLA Modules:
  0.0 951.2 jit_solution(8992065198661120842)
XLA Ops:
  7.2 11.5 %copy.38 = f32[256,32,256]{2,0,1:T(8,128)} copy(f32[256,32,256]{2,1,0:T(8,128)} %param.8) | data formatting | bytes 16777216 | tf_op args[0]
  18.8 36.5 %all-gather.3.cloned.1.call-done = f32[512,32,256]{2,0,1:T(8,128)} async-done(((f32[256,32,256]{2,0,1:T(8,128)}), f32[512,32,256]{2,0,1:T(8,128)}) %all-gather.3.cloned.1.call-update) | async-done | bytes 16777232 | tf_op jit(solution)/shard_map/all_gather | solution.py:35
  55.3 20.5 %convolution_bitcast_fusion = f32[256,512]{1,0:T(8,128)} fusion(f32[512,32,256]{2,0,1:T(8,128)} %all-gather.3.cloned.1.call-done, f32[256,32,256]{2,1,0:T(8,128)} %param.8), kind=kOutput, calls=%fused_computation.8 | convolution fusion | flops 12884901888 | bytes 25690112 | tf_op jit(solution)/shard_map/dot_general | solution.py:37
  75.9 126.3 %all-reduce.7.cloned.1.call-done = f32[256,512]{1,0:T(8,128)} async-done(((f32[256,512]{1,0:T(8,128)}), f32[256,512]{1,0:T(8,128)}) %all-reduce.7.cloned.1.call-update) | async-done | bytes 524304 | tf_op jit(solution)/shard_map/psum | solution.py:38
  205.1 23.3 %all-reduce.9.cloned.1.call-done = f32[128,128]{0,1:T(8,128)} async-done(((f32[128,128]{0,1:T(8,128)}), f32[128,128]{0,1:T(8,128)}) %all-reduce.9.cloned.1.call-update) | async-done | bytes 65552 | tf_op jit(solution)/shard_map/psum | solution.py:42
  230.1 11.7 %cholesky.74 = f32[128,128]{1,0:T(8,128)S(1)} custom-call(f32[128,128]{1,0:T(8,128)S(1)} %fusion.32), custom_call_target="Cholesky" | custom-call | tf_op jit(solution)/shard_map/jit(cholesky)/cholesky | solution.py:14
  243.2 9.8 %custom-call.10 = f32[1,128,128]{1,2,0:T(8,128)S(1)} custom-call(f32[1,128,128]{2,1,0:T(8,128)S(1)} %fusion.21), custom_call_target="InvertDiagBlocksLowerTriangular" | custom-call | tf_op jit(solution)/shard_map/jit(_solve_triangular)/triangular_solve | solution.py:15
  258.3 17.5 %copy.43 = f32[512,32,256]{0,2,1:T(8,128)} copy(f32[512,32,256]{2,0,1:T(8,128)} %all-gather.3.cloned.1.call-done) | data formatting | bytes 33554432 | tf_op jit(solution)/shard_map/all_gather | solution.py:35
  275.8 7.0 all-reduce.11.cloned.1.call-done
  284.6 11.7 %cholesky.85 = f32[128,128]{1,0:T(8,128)S(1)} custom-call(f32[128,128]{1,0:T(8,128)S(1)} %fusion.30), custom_call_target="Cholesky" | custom-call | tf_op jit(solution)/shard_map/jit(cholesky)/cholesky | solution.py:14
  297.6 9.8 %custom-call.11 = f32[1,128,128]{1,2,0:T(8,128)S(1)} custom-call(f32[1,128,128]{2,1,0:T(8,128)S(1)} %fusion.22), custom_call_target="InvertDiagBlocksLowerTriangular" | custom-call | tf_op jit(solution)/shard_map/jit(_solve_triangular)/triangular_solve | solution.py:15
  310.2 20.6 %fusion.4 = f32[64,32,256]{2,0,1:T(8,128)} fusion(f32[512,32,256]{0,2,1:T(8,128)} %copy.43, f32[512,128]{0,1:T(8,128)S(1)} %all_gather.20, s32[]{:T(128)S(6)} %select_n.9), kind=kOutput, calls=%fused_computation.4 | convolution fusion | flops 3221225472 | bytes 19005444 | tf_op jit(solution)/shard_map/dot_general | solution.py:47
  331.1 197.8 %all-gather.5.cloned.1.call-done = f32[64,512,256]{2,0,1:T(8,128)} async-done(((f32[64,32,256]{2,0,1:T(8,128)}), f32[64,512,256]{2,0,1:T(8,128)}) %all-gather.5.cloned.1.call-update) | async-done | bytes 33554448 | tf_op jit(solution)/shard_map/all_gather | solution.py:50
  528.8 58.3 %fusion.10 = f32[32,512]{1,0:T(8,128)} fusion(f32[64,512,256]{2,0,1:T(8,128)} %all-gather.5.cloned.1.call-done, f32[64,32,256]{2,0,1:T(8,128)} %fusion.4), kind=kOutput, calls=%fused_computation.11 | convolution fusion | flops 3221225472 | bytes 35717120 | tf_op jit(solution)/shard_map/dot_general | solution.py:51
  587.2 56.7 %all-reduce.13.cloned.1.call-done = f32[32,512]{1,0:T(8,128)} async-done(((f32[32,512]{1,0:T(8,128)}), f32[32,512]{1,0:T(8,128)}) %all-reduce.13.cloned.1.call-update) | async-done | bytes 65552 | tf_op jit(solution)/shard_map/psum | solution.py:54
  646.3 81.5 %all-reduce.15.cloned.1.call-done = f32[128,128]{0,1:T(8,128)} async-done(((f32[128,128]{0,1:T(8,128)}), f32[128,128]{0,1:T(8,128)}) %all-reduce.15.cloned.1.call-update) | async-done | bytes 65552 | tf_op jit(solution)/shard_map/psum | solution.py:58
  729.6 11.7 %cholesky.96 = f32[128,128]{1,0:T(8,128)S(1)} custom-call(f32[128,128]{1,0:T(8,128)S(1)} %fusion.28), custom_call_target="Cholesky" | custom-call | tf_op jit(solution)/shard_map/jit(cholesky)/cholesky | solution.py:14
  742.6 9.8 %custom-call.12 = f32[1,128,128]{1,2,0:T(8,128)S(1)} custom-call(f32[1,128,128]{2,1,0:T(8,128)S(1)} %fusion.23), custom_call_target="InvertDiagBlocksLowerTriangular" | custom-call | tf_op jit(solution)/shard_map/jit(_solve_triangular)/triangular_solve | solution.py:15
  752.6 17.6 %all_gather.22 = f32[512,128]{1,0:T(8,128)S(1)} all-gather(f32[32,128]{1,0:T(8,128)S(1)} %convolution_bitcast_fusion.4), channel_id=1, replica_groups=mesh['gx'=2,'gy'=16,'gz'=4] {'gy'}, dimensions={0}, use_global_device_ids=true | all-gather | bytes 278528 | tf_op jit(solution)/shard_map/all_gather | solution.py:59
  773.0 84.1 %all-reduce.17.cloned.1.call-done = f32[128,128]{0,1:T(8,128)} async-done(((f32[128,128]{0,1:T(8,128)}), f32[128,128]{0,1:T(8,128)}) %all-reduce.17.cloned.1.call-update) | async-done | bytes 65552 | tf_op jit(solution)/shard_map/psum | solution.py:58
  858.9 11.7 %cholesky.107 = f32[128,128]{1,0:T(8,128)S(1)} custom-call(f32[128,128]{1,0:T(8,128)S(1)} %fusion.26), custom_call_target="Cholesky" | custom-call | tf_op jit(solution)/shard_map/jit(cholesky)/cholesky | solution.py:14
  872.0 9.8 %custom-call.13 = f32[1,128,128]{1,2,0:T(8,128)S(1)} custom-call(f32[1,128,128]{2,1,0:T(8,128)S(1)} %fusion.24), custom_call_target="InvertDiagBlocksLowerTriangular" | custom-call | tf_op jit(solution)/shard_map/jit(_solve_triangular)/triangular_solve | solution.py:15
  882.0 18.0 %all_gather.23 = f32[512,128]{1,0:T(8,128)S(1)} all-gather(f32[32,128]{1,0:T(8,128)S(1)} %convolution_bitcast_fusion.3), channel_id=1, replica_groups=mesh['gx'=2,'gy'=16,'gz'=4] {'gy'}, dimensions={0}, use_global_device_ids=true | all-gather | bytes 278528 | tf_op jit(solution)/shard_map/all_gather | solution.py:61
  899.9 44.0 %fusion.7 = f32[64,8,256]{2,1,0:T(8,128)} fusion(f32[64,512,256]{2,0,1:T(8,128)} %all-gather.5.cloned.1.call-done, f32[512,128]{1,0:T(8,128)S(1)} %all_gather.23, s32[]{:T(128)S(6)} %select_n.10), kind=kOutput, calls=%fused_computation.7 | convolution fusion | flops 805306368 | bytes 34340868 | tf_op jit(solution)/shard_map/dot_general | solution.py:65
  (59 shorter events, 29.3 us)
Async XLA Ops:
  7.2 195.0 %copy-start = (f32[512,128]{1,0:T(8,128)S(1)}, f32[512,128]{1,0:T(8,128)}, u32[]{:S(2)}) copy-start(f32[512,128]{1,0:T(8,128)} %param.9) | copy-start | bytes 786436
  7.2 48.1 %all-gather.3.cloned.1.call-start = ((), (), s32[]{:S(2)}) async-start(), calls=%async_computation | async-start | bytes 25165824 | tf_op jit(solution)/shard_map/all_gather | solution.py:35
  18.7 183.4 %all-reduce.7.cloned.1.call-start = ((), (), s32[]{:S(2)}) async-start(), calls=%async_computation.1 | async-start | bytes 1048576 | tf_op jit(solution)/shard_map/psum | solution.py:38
  75.8 152.5 %all-reduce.9.cloned.1.call-start = ((), (), s32[]{:S(2)}) async-start(), calls=%async_computation.2 | async-start | bytes 131072 | tf_op jit(solution)/shard_map/psum | solution.py:42
  204.8 77.9 %all-reduce.11.cloned.1.call-start = ((), (), s32[]{:S(2)}) async-start(), calls=%async_computation.3 | async-start | bytes 131072 | tf_op jit(solution)/shard_map/psum | solution.py:42
  258.0 270.9 %all-gather.5.cloned.1.call-start = ((), (), s32[]{:S(2)}) async-start(), calls=%async_computation.4 | async-start | bytes 35651584 | tf_op jit(solution)/shard_map/all_gather | solution.py:50
  330.8 313.1 %copy-start.2 = (f32[512,128]{1,0:T(8,128)S(1)}, f32[512,128]{1,0:T(8,128)}, u32[]{:S(2)}) copy-start(f32[512,128]{1,0:T(8,128)} %param.10) | copy-start | bytes 786436
  330.9 313.1 %all-reduce.13.cloned.1.call-start = ((), (), s32[]{:S(2)}) async-start(), calls=%async_computation.5 | async-start | bytes 131072 | tf_op jit(solution)/shard_map/psum | solution.py:54
  587.2 140.6 %all-reduce.15.cloned.1.call-start = ((), (), s32[]{:S(2)}) async-start(), calls=%async_computation.6 | async-start | bytes 131072 | tf_op jit(solution)/shard_map/psum | solution.py:58
  646.0 211.1 %all-reduce.17.cloned.1.call-start = ((), (), s32[]{:S(2)}) async-start(), calls=%async_computation.7 | async-start | bytes 131072 | tf_op jit(solution)/shard_map/psum | solution.py:58
  882.0 62.0 %copy-start.3 = (f32[32,128]{1,0:T(8,128)}, f32[32,128]{1,0:T(8,128)S(1)}, u32[]{:S(2)}) copy-start(f32[32,128]{1,0:T(8,128)S(1)} %convolution_bitcast_fusion.3) | copy-start | bytes 49156
  882.0 62.0 %copy-start.1 = (f32[512,128]{1,0:T(8,128)S(1)}, f32[512,128]{1,0:T(8,128)}, u32[]{:S(2)}) copy-start(f32[512,128]{1,0:T(8,128)} %param.9) | copy-start | bytes 786436
Sparse Core Ops, SparseCore 0:
  18.9 36.4 all-gather.2
  75.9 126.1 all-reduce.6
  205.3 23.0 all-reduce.8
  258.1 24.6 all-reduce.10
  331.0 197.8 all-gather.4
  587.3 56.6 all-reduce.12
  647.7 80.0 all-reduce.14
  772.4 84.6 all-reduce.16
where the time goes:
time: 966 us; the launch traced here: 951 us
  waiting for transfers between devices  613 us (63%)
  matrix products  154 us (16%)
  other arithmetic  94.8 us (10%)
  blocking collectives  40 us (4%)
  local copies, waits for them, and re-layouts  33.5 us (3%)
  between operations  14.8 us (2%)
    all_gather x1, waiting for transfers between devices, body(): kept_two = lax.all_gather(projected, 'gy', axis=1, tiled=True)  198 us
    psum x2, waiting for transfers between devices, body(): lax.psum(value, 'gy')  166 us
    psum x1, waiting for transfers between devices, body(): gram_rows = lax.psum(gram_rows, ('gy', 'gz'))  126 us
    dot_general x1, matrix products, body(): lax.dot_general(projected, kept_two, (((0, 2), (0, 2)), ((), ())), precis...  58.3 us
    psum x1, waiting for transfers between devices, body(): gram_rows_two = lax.psum(gram_rows_two, ('gx', 'gz'))  56.7 us
    another operation x12, other arithmetic, cholesky_step(): factor = jnp.linalg.cholesky(crossed)  49.6 us
    dot_general x1, matrix products, body(): lax.dot_general(own_cols_two, kept_two, (((0,), (1,)), ((), ())), precisi...  44 us
    another operation x8, other arithmetic, cholesky_step(): return jax.scipy.linalg.solve_triangular(factor, product.T, lower=True).T  41.9 us
  transfers between devices with their start and end apart: 8, of which 8 were waited for; matrix products, arithmetic and copies ran while one was open for 2% of the time, Pallas kernels for 0%

commit v1 on v0

v1 whole, which is shorter than its diff:
```python
import functools

import jax
import jax.numpy as jnp
from jax import lax
from jax.experimental import pallas as pl
from jax.experimental.pallas import tpu as pltpu
from jax.sharding import PartitionSpec as P

RANK = 128
ITERS = 2
MESH = pl.DeviceIdType.MESH
f32 = jnp.float32
bf16 = jnp.bfloat16
highest = lax.Precision.HIGHEST
VMEM_LIMIT = 56 * 1024 * 1024


def split(value):
    high = value.astype(bf16)
    return high, (value - high.astype(f32)).astype(bf16)


def dot_nt(a, b, precision=None):
    return lax.dot_general(a, b, (((1,), (1,)), ((), ())), precision=precision, preferred_element_type=f32)


def dot_tn(a, b, precision=None):
    return lax.dot_general(a, b, (((0,), (0,)), ((), ())), precision=precision, preferred_element_type=f32)


def dot_nn(a, b, precision=None):
    return lax.dot_general(a, b, (((1,), (0,)), ((), ())), precision=precision, preferred_element_type=f32)


class Place:
    def __init__(self, plane):
        self.gx, self.gy, self.gz = (lax.axis_index(name) for name in ("gx", "gy", "gz"))
        self.partner = 1 - self.gx
        self.ny, self.nx, self.nz = plane
        self.np = self.ny * self.nx
        self.y, self.x = self.gy // self.nx, self.gy % self.nx

    def plane_peer(self, d):
        dy, dx = d // self.nx, d % self.nx
        return (self.y + dy) % self.ny * self.nx + (self.x + dx) % self.nx

    def plane_source(self, d):
        dy, dx = d // self.nx, d % self.nx
        return (self.y - dy) % self.ny * self.nx + (self.x - dx) % self.nx

    def plane_order(self):
        def hops(d):
            dy, dx = d // self.nx, d % self.nx
            return min(dy, self.ny - dy) + min(dx, self.nx - dx)

        return sorted(range(1, self.np), key=lambda d: (-hops(d), d))

    def z_peer(self, d):
        return (self.gz + d) % self.nz

    def others(self, kinds):
        found = []
        if "x" in kinds:
            found.append({"gx": self.partner})
        if "p" in kinds:
            found += [{"gy": self.plane_peer(d)} for d in range(1, self.np)]
        if "z" in kinds:
            found += [{"gz": self.z_peer(d)} for d in range(1, self.nz)]
        return found

    def greet(self):
        for peer in self.others("pzx"):
            pl.semaphore_signal(pltpu.get_barrier_semaphore(), inc=1, device_id=peer, device_id_type=MESH)

    def meet(self):
        pl.semaphore_wait(pltpu.get_barrier_semaphore(), len(self.others("pzx")))


def remote(src, dst, send_sem, recv_sem, device_id):
    copy = pltpu.make_async_remote_copy(
        src_ref=src, dst_ref=dst, send_sem=send_sem, recv_sem=recv_sem, device_id=device_id, device_id_type=MESH
    )
    copy.start()
    return copy


def sum_scratch(plane, rows, width):
    ny, nx, nz = plane
    planes = ny * nx
    chunk = rows // planes
    dma = pltpu.SemaphoreType.DMA
    return [
        pltpu.VMEM((rows, width), f32),
        pltpu.VMEM((planes, chunk, width), f32),
        pltpu.VMEM((nz, chunk, width), f32),
        pltpu.VMEM((2, rows, width), f32),
        dma((2, planes)),
        dma((2, nz)),
        dma((2, planes)),
        dma((2,)),
    ]


def sum_over_chips(place, total, parts, zparts, whole, rs_sem, z_sem, ag_sem, x_sem):
    chunk = total.shape[0] // place.np
    order = place.plane_order()
    sent = []
    for d in order:
        peer = place.plane_peer(d)
        piece = total.at[pl.ds(pl.multiple_of(peer * chunk, 8), chunk), :]
        sent.append(remote(piece, parts.at[d], rs_sem.at[0, d], rs_sem.at[1, d], {"gy": peer}))
    own = pl.ds(pl.multiple_of(place.gy * chunk, 8), chunk)
    value = total[own, :]
    for d, copy in list(zip(order, sent))[::-1]:
        copy.wait_recv()
        value = value + parts[d]
    zparts[place.gz] = value
    mine = zparts.at[place.gz]
    copies = [
        remote(mine, mine, z_sem.at[0, d], z_sem.at[1, d], {"gz": place.z_peer(d)})
        for d in sorted(range(1, place.nz), key=lambda d: -min(d, place.nz - d))
    ]
    for copy in copies:
        copy.wait_recv()
    value = zparts[0]
    for z in range(1, place.nz):
        value = value + zparts[z]
    whole[place.gx, own, :] = value
    sent += copies
    block = whole.at[place.gx, own, :]
    copies = [remote(block, block, ag_sem.at[0, d], ag_sem.at[1, d], {"gy": place.plane_peer(d)}) for d in order]
    for copy in copies:
        copy.wait_recv()
    mine = whole.at[place.gx]
    last = remote(mine, mine, x_sem.at[0], x_sem.at[1], {"gx": place.partner})
    for copy in sent + copies:
        copy.wait_send()
    last.wait()


def unfold_sum(whole, gram):
    half = whole.shape[2]
    gram[0:half, 0:half] = whole[0, 0:half, :]
    gram[half:, half:] = whole[1, 0:half, :]
    upper = jnp.concatenate([whole[0, half:, :], whole[1, half:, :]], axis=0)
    gram[0:half, half:] = upper
    gram[half:, 0:half] = upper.T


def inverse_factor(crossed):
    n = crossed.shape[0]
    sub = lax.broadcasted_iota(jnp.int32, (8, n), 0)
    lane = lax.broadcasted_iota(jnp.int32, (8, n), 1)
    tiles = [crossed[8 * t : 8 * t + 8, :] for t in range(n // 8)]
    found = []

    def lanes_of(tile, k):
        return jnp.broadcast_to(tile[:, k : k + 1], (8, n))

    def rows_of(tile, k):
        return jnp.broadcast_to(tile[k : k + 1, :], (8, n))

    for t in range(n // 8):
        first = 8 * t
        inside = (lane >= first) & (lane < first + 8)
        columns = [lanes_of(tiles[t], first + k) for k in range(8)]
        block = jnp.where(inside, jnp.where(lane == sub + first, 1.0, 0.0), tiles[t])
        rows = jnp.zeros((8, n), f32)
        for k in range(0, 8, 2):
            one, two = sub == k, sub == k + 1
            fa, fb = columns[k], columns[k + 1]
            a, b, c = rows_of(fa, k), rows_of(fa, k + 1), rows_of(fb, k + 1)
            det = a * c - b * b
            inv = 1.0 / det
            ia, ib, ic = c * inv, b * inv, a * inv
            inv_a = 1.0 / a
            ratio = b * inv_a
            scale_one = lax.rsqrt(a)
            scale_two = lax.rsqrt(det * inv_a)

            def step(value, k=k, fa=fa, fb=fb, ia=ia, ib=ib, ic=ic, one=one, two=two):
                p, q = rows_of(value, k), rows_of(value, k + 1)
                zp, zq = ia * p - ib * q, ic * q - ib * p
                return p, q, jnp.where(one, zp, jnp.where(two, zq, value - fa * zp - fb * zq))

            p, q, block = step(block)
            rows = jnp.where(one, p * scale_one, jnp.where(two, (q - ratio * p) * scale_two, rows))
            for j in range(k + 2, 8):
                columns[j] = step(columns[j])[2]
        found.append(jnp.where(lane < first + 8, rows, 0.0))
        spread = [rows_of(block, k) for k in range(8)]
        for u in range(t + 1, n // 8):
            value = jnp.where(inside, 0.0, tiles[u])
            terms = [lanes_of(tiles[u], first + k) * spread[k] for k in range(8)]
            while len(terms) > 1:
                terms = [a + b for a, b in zip(terms[::2], terms[1::2])]
            tiles[u] = value - terms[0]
    return jnp.concatenate(found, axis=0)


def orthonormal(gram, value):
    for _ in range(ITERS):
        product = dot_nn(gram[...], value, highest)
        crossed = dot_tn(product, product, highest)
        value = dot_nt(product, inverse_factor(crossed), highest)
    return value


def split_block(block, at, pair):
    rows = block.shape[0]
    pair[0:rows, at], pair[rows:, at] = split(block)


def gram_one_sums(place, field, own, other, pair, pair_p, gram, cross, crossed, load_sem, field_sem, cross_sem, total):
    rows, cols, depth = field.shape
    half = cols // 2
    gx, partner = place.gx, place.partner
    step = 8 * depth
    loads = []
    for j in range(cols):
        loads.append(pltpu.make_async_copy(field.at[:, j, :], own.at[j], load_sem.at[j]))
        loads[-1].start()
    place.meet()
    sends = []
    for j in range(half):
        sends.append(
            remote(
                field.at[:, partner * half + j, :], other.at[j], field_sem.at[0, j], field_sem.at[1, j], {"gx": partner}
            )
        )
    gram[...] = jnp.zeros_like(gram)
    for c in range(cols // 8):
        for j in range(8 * c, 8 * c + 8):
            loads[j].wait()
            split_block(own[j], slice(j * depth, (j + 1) * depth), pair)
        at = slice(c * step, (c + 1) * step)
        gram[...] += dot_nt(pair[:, at], pair[0:rows, at])
    cross[...] = jnp.zeros_like(cross)
    for c in range(half // 8):
        for j in range(8 * c, 8 * c + 8):
            sends[j].wait_recv()
            split_block(other[j], slice(j * depth, (j + 1) * depth), pair_p)
        at = slice(c * step, (c + 1) * step)
        mine = pl.ds(pl.multiple_of(gx * half * depth + c * step, step), step)
        both = dot_nt(pair[:, mine], pair_p[0:rows, at])
        cross[...] += both[0:rows] + both[rows:] + dot_nt(pair[0:rows, mine], pair_p[rows:, at])
    value = cross[...]
    cross[...] = jnp.where(gx == 0, value, value.T)
    quarter = rows // 2
    copy = remote(
        cross.at[pl.ds(pl.multiple_of(partner * quarter, 8), quarter), :],
        crossed,
        cross_sem.at[0],
        cross_sem.at[1],
        {"gx": partner},
    )
    total[0:rows, :] = gram[0:rows, :] + gram[rows:, :] + gram[rows:, :].T
    copy.wait_recv()
    total[rows:, :] = cross[pl.ds(pl.multiple_of(gx * quarter, 8), quarter), :] + crossed[...]
    return sends + [copy]


def project(place, pair, basis, partial, arrived, projected, kept, pair_sem, trade_sem, cols, depth):
    gx, gy, partner = place.gx, place.gy, place.partner
    rows = pair.shape[0] // 2
    ranks = RANK // 2
    parts = trade_sem.shape[1]
    each = cols // parts
    _, part_ranks, part_depth = kept.shape
    splits = depth // part_depth
    basis_high, basis_low = split(basis[pl.ds(pl.multiple_of(gx * rows, 8), rows), :].T)
    both = jnp.concatenate([basis_high, basis_low], axis=0)
    here = pl.ds(pl.multiple_of(gx * ranks, 8), ranks)
    there = pl.ds(pl.multiple_of(partner * ranks, 8), ranks)

    def piece(q, peer):
        return projected.at[
            each * q : each * (q + 1),
            pl.ds(pl.multiple_of(peer // splits * part_ranks, 8), part_ranks),
            pl.ds(pl.multiple_of(peer % splits * part_depth, 128), part_depth),
        ]

    def landing(q):
        return kept.at[pl.ds(gy * cols + each * q, each), :, :]

    def partials(q):
        for j in range(each * q, each * (q + 1)):
            at = slice(j * depth, (j + 1) * depth)
            first = dot_nn(both, pair[0:rows, at])
            partial[j] = first[:RANK] + first[RANK:] + dot_nn(basis_high, pair[rows:, at])
        at = slice(each * q, each * (q + 1))
        return remote(partial.at[at, there, :], arrived.at[at], pair_sem.at[0, q], pair_sem.at[1, q], {"gx": partner})

    order = place.plane_order()
    pairs, trades = [partials(0)], {}
    for q in range(parts):
        if q + 1 < parts:
            pairs.append(partials(q + 1))
        pairs[q].wait_recv()
        for j in range(each * q, each * (q + 1)):
            projected[j] = partial[j, here, :] + arrived[j]
        for d in order:
            peer = place.plane_peer(d)
            trades[q, d] = remote(
                piece(q, peer), landing(q), trade_sem.at[0, q, d], trade_sem.at[1, q, d], {"gy": peer}
            )
    local = []
    for q in range(parts):
        local.append(pltpu.make_async_copy(piece(q, gy), landing(q), trade_sem.at[0, q, 0]))
        local[-1].start()
    return pairs, trades, local


def spread_kept(place, kept, kept_pair, peer, cols):
    whole_rows, part_ranks, lanes = kept.shape
    flat = kept.reshape(whole_rows * part_ranks, lanes)
    for r in range(part_ranks):
        value = flat[pl.ds(peer * cols * part_ranks + r, cols, stride=part_ranks), :]
        at = slice(r * lanes, (r + 1) * lanes)
        first = pl.ds(pl.multiple_of(peer * cols, 16), cols)
        second = pl.ds(pl.multiple_of(whole_rows + peer * cols, 16), cols)
        kept_pair[first, at], kept_pair[second, at] = split(value)


def gram_two_sums(place, kept_pair, gram, halves, crossed, cross_sem, total):
    whole_rows = kept_pair.shape[0] // 2
    half = whole_rows // 2
    for k in range(2):
        high = kept_pair[half * k : half * (k + 1), :]
        low = kept_pair[whole_rows + half * k : whole_rows + half * (k + 1), :]
        gram[...] = dot_nt(low, high)
        halves[k, 0:half, :] = dot_nt(high, high)
        halves[k, 0:half, :] += gram[...] + gram[...].T
    high, low = kept_pair[0:half, :], kept_pair[whole_rows : whole_rows + half, :]
    gram[...] = dot_nt(high, kept_pair[half:whole_rows, :])
    gram[...] += dot_nt(low, kept_pair[half:whole_rows, :])
    gram[...] += dot_nt(high, kept_pair[whole_rows + half :, :])
    halves[0, half:, :] = gram[: half // 2, :]
    halves[1, half:, :] = gram[half // 2 :, :]
    copy = remote(halves.at[place.partner], crossed, cross_sem.at[0], cross_sem.at[1], {"gx": place.partner})
    copy.wait_recv()
    total[...] = halves[place.gx] + crossed[...]
    return copy


def kernel(
    plane, field, start_one, start_two, own_one, own_two, core, own, other, pair, pair_p, gram_pair, cross, crossed,
    gram, basis, partial, arrived, projected, kept, kept_pair, square, halves, crossed_two, core_parts, landed,
    load_sem, field_sem, cross_sem, pair_sem, trade_sem, core_sem, *sums
):
    place = Place(plane)
    gx, gy = place.gx, place.gy
    rows, cols, depth = field.shape
    place.greet()
    sums_one, sums_two = sums[: len(sums) // 2], sums[len(sums) // 2 :]
    sent = gram_one_sums(
        place, field, own, other, pair, pair_p, gram_pair, cross, crossed, load_sem, field_sem, cross_sem.at[0], sums_one[0]
    )
    sum_over_chips(place, *sums_one)
    unfold_sum(sums_one[3], gram)
    basis[...] = orthonormal(gram, start_one[...])
    pairs, trades, local = project(
        place, pair, basis, partial, arrived, projected, kept, pair_sem, trade_sem, cols, depth
    )
    own_one[...] = basis[pl.ds(pl.multiple_of(gx * rows, 8), rows), :]
    for copy in local:
        copy.wait()
    spread_kept(place, kept, kept_pair, gy, cols)
    for d in place.plane_order()[::-1]:
        for q in range(len(local)):
            trades[q, d].wait_recv()
        spread_kept(place, kept, kept_pair, place.plane_source(d), cols)
    sent.append(gram_two_sums(place, kept_pair, square, halves, crossed_two, cross_sem.at[1], sums_two[0]))
    sum_over_chips(place, *sums_two)
    unfold_sum(sums_two[3], gram)
    basis[...] = orthonormal(gram, start_two[...])
    own_two[...] = basis[pl.ds(pl.multiple_of(gy * cols, 8), cols), :]

    whole_rows, part_ranks, part_depth = kept.shape
    splits = depth // part_depth
    each = core.shape[1]
    basis_high, basis_low = split(basis[...].T)
    first = dot_nn(jnp.concatenate([basis_high, basis_low], axis=0), kept_pair[0:whole_rows, :])
    first = first[:RANK] + first[RANK:] + dot_nn(basis_high, kept_pair[whole_rows:, :])
    for r in range(part_ranks):
        core_parts[r] = first[:, r * part_depth : (r + 1) * part_depth]
    landing = landed.at[
        pl.ds(gy // splits * part_ranks, part_ranks),
        :,
        pl.ds(pl.multiple_of(gy % splits * part_depth, 128), part_depth),
    ]

    def piece(peer):
        return core_parts.at[:, pl.ds(pl.multiple_of(peer * each, 8), each), :]

    last = []
    for d in place.plane_order():
        peer = place.plane_peer(d)
        last.append(remote(piece(peer), landing, core_sem.at[0, d], core_sem.at[1, d], {"gy": peer}))
    stays = pltpu.make_async_copy(piece(gy), landing, core_sem.at[0, 0])
    stays.start()
    for copy in sent + pairs + list(trades.values()):
        copy.wait_send()
    stays.wait()
    for copy in last:
        copy.wait_recv()
    core[...] = landed[...]
    for copy in last:
        copy.wait_send()


PARTS = 4


def body(plane, field, start_one, start_two):
    rows, cols, depth = field.shape
    ny, nx, nz = plane
    planes = ny * nx
    splits = depth // 128
    part_ranks = RANK // 2 // (planes // splits)
    whole_rows = planes * cols
    half = whole_rows // 2
    dma = pltpu.SemaphoreType.DMA
    vmem = pl.BlockSpec(memory_space=pltpu.VMEM)
    core_shape = (RANK // 2, RANK // planes, depth)
    size = max(2 * rows, whole_rows)
    return pl.pallas_call(
        functools.partial(kernel, plane),
        out_shape=(
            jax.ShapeDtypeStruct((rows, RANK), f32),
            jax.ShapeDtypeStruct((cols, RANK), f32),
            jax.ShapeDtypeStruct(core_shape, f32),
        ),
        in_specs=[pl.BlockSpec(memory_space=pl.ANY), vmem, vmem],
        out_specs=(vmem, vmem, vmem),
        scratch_shapes=[
            pltpu.VMEM((cols, rows, depth), f32),
            pltpu.VMEM((cols // 2, rows, depth), f32),
            pltpu.VMEM((2 * rows, cols * depth), bf16),
            pltpu.VMEM((2 * rows, cols // 2 * depth), bf16),
            pltpu.VMEM((2 * rows, rows), f32),
            pltpu.VMEM((rows, rows), f32),
            pltpu.VMEM((rows // 2, rows), f32),
            pltpu.VMEM((size, size), f32),
            pltpu.VMEM((size, RANK), f32),
            pltpu.VMEM((cols, RANK, depth), f32),
            pltpu.VMEM((cols, RANK // 2, depth), f32),
            pltpu.VMEM((cols, RANK // 2, depth), f32),
            pltpu.VMEM((whole_rows, part_ranks, 128), f32),
            pltpu.VMEM((2 * whole_rows, part_ranks * 128), bf16),
            pltpu.VMEM((half, half), f32),
            pltpu.VMEM((2, half * 3 // 2, half), f32),
            pltpu.VMEM((half * 3 // 2, half), f32),
            pltpu.VMEM((part_ranks, RANK, 128), f32),
            pltpu.VMEM(core_shape, f32),
            dma((cols,)),
            dma((2, cols // 2)),
            dma((2, 2)),
            dma((2, PARTS)),
            dma((2, PARTS, planes)),
            dma((2, planes)),
            *sum_scratch(plane, rows * 3 // 2, rows),
            *sum_scratch(plane, half * 3 // 2, half),
        ],
        compiler_params=pltpu.CompilerParams(collective_id=0, has_side_effects=True, vmem_limit_bytes=VMEM_LIMIT),
        name="hosvd",
    )(field, start_one, start_two)


def solution(mesh):
    sizes = dict(mesh.shape)
    side = 4 if sizes["gy"] == 16 else 2
    plane = (sizes["gy"] // side, side, sizes["gz"])
    return jax.shard_map(
        functools.partial(body, plane),
        mesh=mesh,
        in_specs=(P("gx", "gy", "gz"), P(), P()),
        out_specs=(P("gx", None), P("gy", None), P("gx", "gy", "gz")),
        check_vma=False,
    )
```

time: 966 us -> 138 us (0.14); the launches traced: 951 us -> 138 us
  waiting for transfers between devices: 613 us -> 0 us
  matrix products: 154 us -> 0 us
  Pallas kernels: 0 us -> 133 us
  other arithmetic: 94.8 us -> 0 us
  blocking collectives: 40 us -> 0 us
  local copies, waits for them, and re-layouts: 33.5 us -> 4.76 us
  between operations: 14.8 us -> 0.64 us
    psum x6 -> x0, waiting for transfers between devices: 379 us -> none  [the longest x2 166 us: body(): lax.psum(value, 'gy')]
    all_gather x2 -> x0, waiting for transfers between devices: 234 us -> none  [the longest x1 198 us: body(): kept_two = lax.all_gather(projected, 'gy', axis=1, tiled=True)]
    dot_general x12 -> x0, matrix products: 153 us -> none  [the longest x1 58.3 us: body(): lax.dot_general(projected, kept_two, (((0, 2), (0, 2)), ((), ())), precis...]
    pallas_call x0 -> x1, Pallas kernels: none -> 133 us  [body(): pl.pallas_call(functools.partial(kernel, plane), out_shape=(jax.ShapeDtyp...]
    another operation x20 -> x0, other arithmetic: 91.4 us -> none  [the longest x12 49.6 us: cholesky_step(): factor = jnp.linalg.cholesky(crossed)]
    all_gather x4 -> x0, blocking collectives: 40 us -> none  [the longest x1 18 us: body(): whole_two = lax.all_gather(local_two, 'gy', axis=0, tiled=True)]
    all_gather x1 -> x0, local copies, waits for them, and re-layouts: 17.5 us -> none  [body(): kept_one = lax.all_gather(field, 'gx', axis=0, tiled=True)]
  transfers between devices with their start and end apart: 8 -> 0, of which waited for: 8 -> 0; matrix products, arithmetic and copies ran while one was open for 2% -> 0% of each run, Pallas kernels for 0% -> 0%
where the time goes in v1:
time: 138 us
  Pallas kernels  133 us (96%)
  local copies, waits for them, and re-layouts  4.76 us (3%)
    pallas_call x1, Pallas kernels, body(): pl.pallas_call(functools.partial(kernel, plane), out_shape=(jax.ShapeDtyp...  133 us
    unnamed x3, local copies, waits for them, and re-layouts  4.76 us

profile of v1, /device:TPU:1, one launch (start us, length us, event | category | flops | bytes accessed | tf_op | source)
XLA Modules:
  0.0 138.2 jit_solution(16542001152788378356)
XLA Ops:
  0.6 132.8 %hosvd.1 = (f32[256,128]{1,0:T(8,128)}, f32[32,128]{1,0:T(8,128)}, f32[64,8,256]{2,1,0:T(8,128)}) custom-call(f32[256,32,256]{2,1,0:T(8,128)} %field.1, f32[512,128]{1,0:T(8,128)} %start_one.1, f32[512,128]{1,0:T(8,128)} %start_two.1), custom_call_target="tpu_custom_call" | custom-call | tf_op jit(solution)/shard_map/hosvd/pallas_call | solution.py:428
  133.4 1.6 %copy.9 = f32[256,128]{1,0:T(8,128)} copy(f32[256,128]{1,0:T(8,128)} %get-tuple-element.6) | data formatting | bytes 262144
  135.0 1.3 copy.10
  136.3 1.9 %copy.11 = f32[64,8,256]{2,1,0:T(8,128)} copy(f32[64,8,256]{2,1,0:T(8,128)} %get-tuple-element.8) | data formatting | bytes 1048576

commit v2 on v1

--- a/solution.py
+++ b/solution.py
@@ -139,16 +139,63 @@
     last.wait()
 
 
-def unfold_sum(whole, gram):
+def unfold_sum(whole, terms):
     half = whole.shape[2]
-    gram[0:half, 0:half] = whole[0, 0:half, :]
-    gram[half:, half:] = whole[1, 0:half, :]
     upper = jnp.concatenate([whole[0, half:, :], whole[1, half:, :]], axis=0)
-    gram[0:half, half:] = upper
-    gram[half:, 0:half] = upper.T
-
-
-def inverse_factor(crossed):
+    first, second = slice(0, half), slice(half, 2 * half)
+    blocks = {
+        (first, first): whole[0, 0:half, :],
+        (second, second): whole[1, 0:half, :],
+        (first, second): upper,
+        (second, first): upper.T,
+    }
+    for (rows, cols), block in blocks.items():
+        terms[0, rows, cols], terms[1, rows, cols], terms[2, rows, cols] = split3(block)
+
+
+def small_inverse_factor(entry):
+    n = len(entry)
+    entry = [list(row) for row in entry]
+    below = [[None] * n for _ in range(n)]
+    result = [[None] * (i + 1) for i in range(n)]
+    for k in range(0, n, 2):
+        a, b, c = entry[k][k], entry[k + 1][k], entry[k + 1][k + 1]
+        det = a * c - b * b
+        inverse = reciprocal(det)
+        over = 1.0 / a
+        ratio = b * over
+        scale_one, scale_two = lax.rsqrt(a), lax.rsqrt(det * over)
+        for j in range(k):
+            result[k][j] = below[k][j] * scale_one
+            result[k + 1][j] = (below[k + 1][j] - ratio * below[k][j]) * scale_two
+        result[k][k] = scale_one
+        result[k + 1][k] = -ratio * scale_two
+        result[k + 1][k + 1] = scale_two
+        factors = {}
+        for i in range(k + 2, n):
+            p, q = entry[i][k], entry[i][k + 1]
+            factors[i] = (c * p - b * q) * inverse, (a * q - b * p) * inverse
+        for i in range(k + 2, n):
+            f, g = factors[i]
+            for j in range(k + 2, i + 1):
+                entry[i][j] = entry[i][j] - (f * entry[j][k] + g * entry[j][k + 1])
+            for j in range(k):
+                below[i][j] = below[i][j] - (f * below[k][j] + g * below[k + 1][j])
+            below[i][k], below[i][k + 1] = -f, -g
+    return result
+
+
+def reciprocal(value):
+    return 1.0 / value
+
+
+def tree(terms):
+    while len(terms) > 1:
+        terms = [a + b for a, b in zip(terms[::2], terms[1::2])] + ([terms[-1]] if len(terms) % 2 else [])
+    return terms[0]
+
+
+def inverse_factor(crossed, held):
     n = crossed.shape[0]
     sub = lax.broadcasted_iota(jnp.int32, (8, n), 0)
     lane = lax.broadcasted_iota(jnp.int32, (8, n), 1)
@@ -158,53 +205,62 @@
     def lanes_of(tile, k):
         return jnp.broadcast_to(tile[:, k : k + 1], (8, n))
 
-    def rows_of(tile, k):
-        return jnp.broadcast_to(tile[k : k + 1, :], (8, n))
+    def row_of(t, which, k):
+        return jnp.broadcast_to(held[t, which, k : k + 1, :], (8, n))
 
     for t in range(n // 8):
         first = 8 * t
         inside = (lane >= first) & (lane < first + 8)
-        columns = [lanes_of(tiles[t], first + k) for k in range(8)]
-        block = jnp.where(inside, jnp.where(lane == sub + first, 1.0, 0.0), tiles[t])
-        rows = jnp.zeros((8, n), f32)
-        for k in range(0, 8, 2):
-            one, two = sub == k, sub == k + 1
-            fa, fb = columns[k], columns[k + 1]
-            a, b, c = rows_of(fa, k), rows_of(fa, k + 1), rows_of(fb, k + 1)
-            det = a * c - b * b
-            inv = 1.0 / det
-            ia, ib, ic = c * inv, b * inv, a * inv
-            inv_a = 1.0 / a
-            ratio = b * inv_a
-            scale_one = lax.rsqrt(a)
-            scale_two = lax.rsqrt(det * inv_a)
-
-            def step(value, k=k, fa=fa, fb=fb, ia=ia, ib=ib, ic=ic, one=one, two=two):
-                p, q = rows_of(value, k), rows_of(value, k + 1)
-                zp, zq = ia * p - ib * q, ic * q - ib * p
-                return p, q, jnp.where(one, zp, jnp.where(two, zq, value - fa * zp - fb * zq))
-
-            p, q, block = step(block)
-            rows = jnp.where(one, p * scale_one, jnp.where(two, (q - ratio * p) * scale_two, rows))
-            for j in range(k + 2, 8):
-                columns[j] = step(columns[j])[2]
-        found.append(jnp.where(lane < first + 8, rows, 0.0))
-        spread = [rows_of(block, k) for k in range(8)]
+        for k in range(8):
+            held[t, k] = lanes_of(tiles[t], first + k)
+        held[t, 8] = jnp.where(inside, jnp.where(lane == sub + first, 1.0, 0.0), tiles[t])
+        factor = small_inverse_factor([[row_of(t, j, i) for j in range(i + 1)] for i in range(8)])
+        spread = [row_of(t, 8, k) for k in range(8)]
+        rows = [tree([factor[i][j] * spread[j] for j in range(i + 1)]) for i in range(8)]
+        value = rows[0]
+        for i in range(1, 8):
+            value = jnp.where(sub == i, rows[i], value)
+        found.append(jnp.where(lane < first + 8, value, 0.0))
+        if t + 1 == n // 8:
+            break
+        solved = [tree([factor[i][k] * rows[i] for i in range(k, 8)]) for k in range(8)]
         for u in range(t + 1, n // 8):
-            value = jnp.where(inside, 0.0, tiles[u])
-            terms = [lanes_of(tiles[u], first + k) * spread[k] for k in range(8)]
-            while len(terms) > 1:
-                terms = [a + b for a, b in zip(terms[::2], terms[1::2])]
-            tiles[u] = value - terms[0]
+            terms = [lanes_of(tiles[u], first + k) * solved[k] for k in range(8)]
+            tiles[u] = jnp.where(inside, 0.0, tiles[u]) - tree(terms)
     return jnp.concatenate(found, axis=0)
 
 
-def orthonormal(gram, value):
-    for _ in range(ITERS):
-        product = dot_nn(gram[...], value, highest)
-        crossed = dot_tn(product, product, highest)
-        value = dot_nt(product, inverse_factor(crossed), highest)
-    return value
+def split3(value):
+    high = value.astype(bf16)
+    rest = value - high.astype(f32)
+    middle = rest.astype(bf16)
+    return high, middle, (rest - middle.astype(f32)).astype(bf16)
+
+
+def times(left, right):
+    n = left.shape[0]
+    high, middle, low = split3(left)
+    one = dot_nn(jnp.concatenate([high, middle, low], axis=0), right[0])
+    two = dot_nn(jnp.concatenate([high, middle], axis=0), right[1])
+    three = dot_nn(high, right[2])
+    return one[:n] + (one[n : 2 * n] + two[:n]) + (one[2 * n :] + two[n:] + three)
+
+
+def square(rows):
+    n = rows.shape[0]
+    high, middle, low = split3(rows)
+    one = dot_nt(jnp.concatenate([high, middle, low], axis=0), high)
+    mid, last = one[n : 2 * n], one[2 * n :]
+    return one[:n] + (mid + mid.T) + (last + last.T + dot_nt(middle, middle))
+
+
+def orthonormal(terms, start, held):
+    assert ITERS == 2
+    product = times(start, terms)
+    inverse = inverse_factor(square(product), held)
+    second = times(product, terms)
+    product = times(inverse, split3(second))
+    return times(inverse_factor(square(product), held), split3(product))
 
 
 def split_block(block, at, pair):
@@ -221,21 +277,26 @@
     for j in range(cols):
         loads.append(pltpu.make_async_copy(field.at[:, j, :], own.at[j], load_sem.at[j]))
         loads[-1].start()
-    place.meet()
+    gram[...] = jnp.zeros_like(gram)
     sends = []
-    for j in range(half):
-        sends.append(
-            remote(
-                field.at[:, partner * half + j, :], other.at[j], field_sem.at[0, j], field_sem.at[1, j], {"gx": partner}
-            )
-        )
-    gram[...] = jnp.zeros_like(gram)
     for c in range(cols // 8):
         for j in range(8 * c, 8 * c + 8):
             loads[j].wait()
             split_block(own[j], slice(j * depth, (j + 1) * depth), pair)
         at = slice(c * step, (c + 1) * step)
         gram[...] += dot_nt(pair[:, at], pair[0:rows, at])
+        if c == 0:
+            place.meet()
+            for j in range(half):
+                sends.append(
+                    remote(
+                        field.at[:, partner * half + j, :],
+                        other.at[j],
+                        field_sem.at[0, j],
+                        field_sem.at[1, j],
+                        {"gx": partner},
+                    )
+                )
     cross[...] = jnp.zeros_like(cross)
     for c in range(half // 8):
         for j in range(8 * c, 8 * c + 8):
@@ -269,7 +330,7 @@
     each = cols // parts
     _, part_ranks, part_depth = kept.shape
     splits = depth // part_depth
-    basis_high, basis_low = split(basis[pl.ds(pl.multiple_of(gx * rows, 8), rows), :].T)
+    basis_high, basis_low = split(basis[:, pl.ds(pl.multiple_of(gx * rows, 128), rows)])
     both = jnp.concatenate([basis_high, basis_low], axis=0)
     here = pl.ds(pl.multiple_of(gx * ranks, 8), ranks)
     there = pl.ds(pl.multiple_of(partner * ranks, 8), ranks)
@@ -346,24 +407,26 @@
 
 def kernel(
     plane, field, start_one, start_two, own_one, own_two, core, own, other, pair, pair_p, gram_pair, cross, crossed,
-    gram, basis, partial, arrived, projected, kept, kept_pair, square, halves, crossed_two, core_parts, landed,
+    terms, basis, start, turned, held, partial, arrived, projected, kept, kept_pair, square, halves, crossed_two, core_parts, landed,
     load_sem, field_sem, cross_sem, pair_sem, trade_sem, core_sem, *sums
 ):
     place = Place(plane)
     gx, gy = place.gx, place.gy
     rows, cols, depth = field.shape
     place.greet()
+    start[0] = start_one[...].T
+    start[1] = start_two[...].T
     sums_one, sums_two = sums[: len(sums) // 2], sums[len(sums) // 2 :]
     sent = gram_one_sums(
         place, field, own, other, pair, pair_p, gram_pair, cross, crossed, load_sem, field_sem, cross_sem.at[0], sums_one[0]
     )
     sum_over_chips(place, *sums_one)
-    unfold_sum(sums_one[3], gram)
-    basis[...] = orthonormal(gram, start_one[...])
+    unfold_sum(sums_one[3], terms)
+    basis[...] = orthonormal(terms, start[0], held)
     pairs, trades, local = project(
         place, pair, basis, partial, arrived, projected, kept, pair_sem, trade_sem, cols, depth
     )
-    own_one[...] = basis[pl.ds(pl.multiple_of(gx * rows, 8), rows), :]
+    own_one[...] = basis[:, pl.ds(pl.multiple_of(gx * rows, 128), rows)].T
     for copy in local:
         copy.wait()
     spread_kept(place, kept, kept_pair, gy, cols)
@@ -373,14 +436,12 @@
         spread_kept(place, kept, kept_pair, place.plane_source(d), cols)
     sent.append(gram_two_sums(place, kept_pair, square, halves, crossed_two, cross_sem.at[1], sums_two[0]))
     sum_over_chips(place, *sums_two)
-    unfold_sum(sums_two[3], gram)
-    basis[...] = orthonormal(gram, start_two[...])
-    own_two[...] = basis[pl.ds(pl.multiple_of(gy * cols, 8), cols), :]
-
+    unfold_sum(sums_two[3], terms)
+    basis[...] = orthonormal(terms, start[1], held)
     whole_rows, part_ranks, part_depth = kept.shape
     splits = depth // part_depth
     each = core.shape[1]
-    basis_high, basis_low = split(basis[...].T)
+    basis_high, basis_low = split(basis[...])
     first = dot_nn(jnp.concatenate([basis_high, basis_low], axis=0), kept_pair[0:whole_rows, :])
     first = first[:RANK] + first[RANK:] + dot_nn(basis_high, kept_pair[whole_rows:, :])
     for r in range(part_ranks):
@@ -400,6 +461,8 @@
         last.append(remote(piece(peer), landing, core_sem.at[0, d], core_sem.at[1, d], {"gy": peer}))
     stays = pltpu.make_async_copy(piece(gy), landing, core_sem.at[0, 0])
     stays.start()
+    turned[...] = basis[...].T
+    own_two[...] = turned[pl.ds(pl.multiple_of(gy * cols, 8), cols), :]
     for copy in sent + pairs + list(trades.values()):
         copy.wait_send()
     stays.wait()
@@ -408,6 +471,16 @@
     core[...] = landed[...]
     for copy in last:
         copy.wait_send()
+
+
+def deliver(*refs):
+    count = len(refs) // 2
+    sem = refs[-1]
+    copies = [pltpu.make_async_copy(refs[k], refs[count + k], sem.at[k]) for k in range(count)]
+    for copy in copies:
+        copy.start()
+    for copy in copies:
+        copy.wait()
 
 
 PARTS = 4
@@ -425,7 +498,7 @@
     vmem = pl.BlockSpec(memory_space=pltpu.VMEM)
     core_shape = (RANK // 2, RANK // planes, depth)
     size = max(2 * rows, whole_rows)
-    return pl.pallas_call(
+    outs = pl.pallas_call(
         functools.partial(kernel, plane),
         out_shape=(
             jax.ShapeDtypeStruct((rows, RANK), f32),
@@ -442,8 +515,11 @@
             pltpu.VMEM((2 * rows, rows), f32),
             pltpu.VMEM((rows, rows), f32),
             pltpu.VMEM((rows // 2, rows), f32),
-            pltpu.VMEM((size, size), f32),
+            pltpu.VMEM((3, size, size), bf16),
+            pltpu.VMEM((RANK, size), f32),
+            pltpu.VMEM((2, RANK, size), f32),
             pltpu.VMEM((size, RANK), f32),
+            pltpu.VMEM((RANK // 8, 9, 8, RANK), f32),
             pltpu.VMEM((cols, RANK, depth), f32),
             pltpu.VMEM((cols, RANK // 2, depth), f32),
             pltpu.VMEM((cols, RANK // 2, depth), f32),
@@ -466,6 +542,15 @@
         compiler_params=pltpu.CompilerParams(collective_id=0, has_side_effects=True, vmem_limit_bytes=VMEM_LIMIT),
         name="hosvd",
     )(field, start_one, start_two)
+    anywhere = pl.BlockSpec(memory_space=pl.ANY)
+    return pl.pallas_call(
+        deliver,
+        out_shape=tuple(jax.ShapeDtypeStruct(out.shape, f32) for out in outs),
+        in_specs=[anywhere] * len(outs),
+        out_specs=(anywhere,) * len(outs),
+        scratch_shapes=[dma((len(outs),))],
+        name="deliver",
+    )(*outs)
 
 
 def solution(mesh):

time: 138 us -> 140 us (1.014)
  Pallas kernels: 133 us -> 139 us
  local copies, waits for them, and re-layouts: 4.76 us -> 0 us
    pallas_call x0 -> x1, Pallas kernels: none -> 21.5 us  [body(): pl.pallas_call(deliver, out_shape=tuple((jax.ShapeDtypeStruct(out.shape,...]
    pallas_call x1, Pallas kernels: 133 us -> 117 us  [body(): pl.pallas_call(functools.partial(kernel, plane), out_shape=(jax.ShapeDtyp...]
    unnamed x3 -> x0, local copies, waits for them, and re-layouts: 4.76 us -> none
where the time goes in v2:
time: 140 us
  Pallas kernels  139 us (99%)
    pallas_call x1, Pallas kernels, body(): pl.pallas_call(functools.partial(kernel, plane), out_shape=(jax.ShapeDtyp...  117 us
    pallas_call x1, Pallas kernels, body(): pl.pallas_call(deliver, out_shape=tuple((jax.ShapeDtypeStruct(out.shape,...  21.5 us

profile of v2, /device:TPU:1, one launch (start us, length us, event | category | flops | bytes accessed | tf_op | source)
XLA Modules:
  0.0 139.7 jit_solution(873754917154065013)
XLA Ops:
  0.6 117.4 %hosvd.1 = (f32[256,128]{1,0:T(8,128)}, f32[32,128]{1,0:T(8,128)}, f32[64,8,256]{2,1,0:T(8,128)}) custom-call(f32[256,32,256]{2,1,0:T(8,128)} %field.1, f32[512,128]{1,0:T(8,128)} %start_one.1, f32[512,128]{1,0:T(8,128)} %start_two.1), custom_call_target="tpu_custom_call" | custom-call | tf_op jit(solution)/shard_map/hosvd/pallas_call | solution.py:501
  118.1 21.5 %deliver.1 = (f32[256,128]{1,0:T(8,128)}, f32[32,128]{1,0:T(8,128)}, f32[64,8,256]{2,1,0:T(8,128)}) custom-call(f32[256,128]{1,0:T(8,128)} %get-tuple-element.6.refs_0_, f32[32,128]{1,0:T(8,128)} %get-tuple-element.7.refs_1_, f32[64,8,256]{2,1,0:T(8,128)} %get-tuple-element.8.refs_2_), custom_call_target="tpu_custom_call" | custom-call | tf_op jit(solution)/shard_map/deliver/pallas_call | solution.py:546

commit v3 on v2

--- a/solution.py
+++ b/solution.py
@@ -326,8 +326,8 @@
     gx, gy, partner = place.gx, place.gy, place.partner
     rows = pair.shape[0] // 2
     ranks = RANK // 2
-    parts = trade_sem.shape[1]
-    each = cols // parts
+    sizes = parts_of(cols)
+    spans = [slice(sum(sizes[:q]), sum(sizes[: q + 1])) for q in range(len(sizes))]
     _, part_ranks, part_depth = kept.shape
     splits = depth // part_depth
     basis_high, basis_low = split(basis[:, pl.ds(pl.multiple_of(gx * rows, 128), rows)])
@@ -337,29 +337,29 @@
 
     def piece(q, peer):
         return projected.at[
-            each * q : each * (q + 1),
+            spans[q],
             pl.ds(pl.multiple_of(peer // splits * part_ranks, 8), part_ranks),
             pl.ds(pl.multiple_of(peer % splits * part_depth, 128), part_depth),
         ]
 
     def landing(q):
-        return kept.at[pl.ds(gy * cols + each * q, each), :, :]
+        return kept.at[pl.ds(gy * cols + spans[q].start, sizes[q]), :, :]
 
     def partials(q):
-        for j in range(each * q, each * (q + 1)):
+        for j in range(spans[q].start, spans[q].stop):
             at = slice(j * depth, (j + 1) * depth)
             first = dot_nn(both, pair[0:rows, at])
             partial[j] = first[:RANK] + first[RANK:] + dot_nn(basis_high, pair[rows:, at])
-        at = slice(each * q, each * (q + 1))
+        at = spans[q]
         return remote(partial.at[at, there, :], arrived.at[at], pair_sem.at[0, q], pair_sem.at[1, q], {"gx": partner})
 
     order = place.plane_order()
     pairs, trades = [partials(0)], {}
-    for q in range(parts):
-        if q + 1 < parts:
+    for q in range(len(sizes)):
+        if q + 1 < len(sizes):
             pairs.append(partials(q + 1))
         pairs[q].wait_recv()
-        for j in range(each * q, each * (q + 1)):
+        for j in range(spans[q].start, spans[q].stop):
             projected[j] = partial[j, here, :] + arrived[j]
         for d in order:
             peer = place.plane_peer(d)
@@ -367,7 +367,7 @@
                 piece(q, peer), landing(q), trade_sem.at[0, q, d], trade_sem.at[1, q, d], {"gy": peer}
             )
     local = []
-    for q in range(parts):
+    for q in range(len(sizes)):
         local.append(pltpu.make_async_copy(piece(q, gy), landing(q), trade_sem.at[0, q, 0]))
         local[-1].start()
     return pairs, trades, local
@@ -430,7 +430,7 @@
     for copy in local:
         copy.wait()
     spread_kept(place, kept, kept_pair, gy, cols)
-    for d in place.plane_order()[::-1]:
+    for d in place.plane_order():
         for q in range(len(local)):
             trades[q, d].wait_recv()
         spread_kept(place, kept, kept_pair, place.plane_source(d), cols)
@@ -442,30 +442,37 @@
     splits = depth // part_depth
     each = core.shape[1]
     basis_high, basis_low = split(basis[...])
-    first = dot_nn(jnp.concatenate([basis_high, basis_low], axis=0), kept_pair[0:whole_rows, :])
-    first = first[:RANK] + first[RANK:] + dot_nn(basis_high, kept_pair[whole_rows:, :])
-    for r in range(part_ranks):
-        core_parts[r] = first[:, r * part_depth : (r + 1) * part_depth]
-    landing = landed.at[
-        pl.ds(gy // splits * part_ranks, part_ranks),
-        :,
-        pl.ds(pl.multiple_of(gy % splits * part_depth, 128), part_depth),
-    ]
-
-    def piece(peer):
-        return core_parts.at[:, pl.ds(pl.multiple_of(peer * each, 8), each), :]
-
+    both = jnp.concatenate([basis_high, basis_low], axis=0)
+    order = place.plane_order()
     last = []
-    for d in place.plane_order():
-        peer = place.plane_peer(d)
-        last.append(remote(piece(peer), landing, core_sem.at[0, d], core_sem.at[1, d], {"gy": peer}))
-    stays = pltpu.make_async_copy(piece(gy), landing, core_sem.at[0, 0])
-    stays.start()
+    for q in range(2):
+        ranks = part_ranks // 2
+        at = slice(q * ranks * part_depth, (q + 1) * ranks * part_depth)
+        first = dot_nn(both, kept_pair[0:whole_rows, at])
+        first = first[:RANK] + first[RANK:] + dot_nn(basis_high, kept_pair[whole_rows:, at])
+        for r in range(ranks):
+            core_parts[q * ranks + r] = first[:, r * part_depth : (r + 1) * part_depth]
+        landing = landed.at[
+            pl.ds(gy // splits * part_ranks + q * ranks, ranks),
+            :,
+            pl.ds(pl.multiple_of(gy % splits * part_depth, 128), part_depth),
+        ]
+
+        def piece(peer, q=q, ranks=ranks):
+            return core_parts.at[q * ranks : (q + 1) * ranks, pl.ds(pl.multiple_of(peer * each, 8), each), :]
+
+        for d in order:
+            peer = place.plane_peer(d)
+            last.append(remote(piece(peer), landing, core_sem.at[0, q, d], core_sem.at[1, q, d], {"gy": peer}))
+        stays = pltpu.make_async_copy(piece(gy), landing, core_sem.at[0, q, 0])
+        stays.start()
+        local.append(stays)
     turned[...] = basis[...].T
     own_two[...] = turned[pl.ds(pl.multiple_of(gy * cols, 8), cols), :]
     for copy in sent + pairs + list(trades.values()):
         copy.wait_send()
-    stays.wait()
+    for copy in local[-2:]:
+        copy.wait()
     for copy in last:
         copy.wait_recv()
     core[...] = landed[...]
@@ -475,15 +482,12 @@
 
 def deliver(*refs):
     count = len(refs) // 2
-    sem = refs[-1]
-    copies = [pltpu.make_async_copy(refs[k], refs[count + k], sem.at[k]) for k in range(count)]
-    for copy in copies:
-        copy.start()
-    for copy in copies:
-        copy.wait()
-
-
-PARTS = 4
+    for k in range(count):
+        refs[count + k][...] = refs[k][...]
+
+
+def parts_of(cols):
+    return [cols // 8, cols // 8, cols // 4, cols // 2]
 
 
 def body(plane, field, start_one, start_two):
@@ -494,6 +498,7 @@
     part_ranks = RANK // 2 // (planes // splits)
     whole_rows = planes * cols
     half = whole_rows // 2
+    parts = len(parts_of(cols))
     dma = pltpu.SemaphoreType.DMA
     vmem = pl.BlockSpec(memory_space=pltpu.VMEM)
     core_shape = (RANK // 2, RANK // planes, depth)
@@ -533,22 +538,20 @@
             dma((cols,)),
             dma((2, cols // 2)),
             dma((2, 2)),
-            dma((2, PARTS)),
-            dma((2, PARTS, planes)),
-            dma((2, planes)),
+            dma((2, parts)),
+            dma((2, parts, planes)),
+            dma((2, 2, planes)),
             *sum_scratch(plane, rows * 3 // 2, rows),
             *sum_scratch(plane, half * 3 // 2, half),
         ],
         compiler_params=pltpu.CompilerParams(collective_id=0, has_side_effects=True, vmem_limit_bytes=VMEM_LIMIT),
         name="hosvd",
     )(field, start_one, start_two)
-    anywhere = pl.BlockSpec(memory_space=pl.ANY)
     return pl.pallas_call(
         deliver,
         out_shape=tuple(jax.ShapeDtypeStruct(out.shape, f32) for out in outs),
-        in_specs=[anywhere] * len(outs),
-        out_specs=(anywhere,) * len(outs),
-        scratch_shapes=[dma((len(outs),))],
+        in_specs=[vmem] * len(outs),
+        out_specs=(vmem,) * len(outs),
         name="deliver",
     )(*outs)
 

time: 140 us -> 120 us (0.86)
  Pallas kernels: 139 us -> 119 us
    pallas_call x1, Pallas kernels: 21.5 us -> 1.98 us  [body(): pl.pallas_call(deliver, out_shape=tuple((jax.ShapeDtypeStruct(out.shape,...]
where the time goes in v3:
time: 120 us
  Pallas kernels  119 us (99%)
    pallas_call x1, Pallas kernels, body(): pl.pallas_call(functools.partial(kernel, plane), out_shape=(jax.ShapeDtyp...  117 us

profile of v3, /device:TPU:1, one launch (start us, length us, event | category | flops | bytes accessed | tf_op | source)
XLA Modules:
  0.0 119.7 jit_solution(12543545229000668521)
XLA Ops:
  0.6 117.1 %hosvd.1 = (f32[256,128]{1,0:T(8,128)}, f32[32,128]{1,0:T(8,128)}, f32[64,8,256]{2,1,0:T(8,128)}) custom-call(f32[256,32,256]{2,1,0:T(8,128)} %field.1, f32[512,128]{1,0:T(8,128)} %start_one.1, f32[512,128]{1,0:T(8,128)} %start_two.1), custom_call_target="tpu_custom_call" | custom-call | tf_op jit(solution)/shard_map/hosvd/pallas_call | solution.py:506
  117.7 2.0 %deliver.1 = (f32[256,128]{1,0:T(8,128)}, f32[32,128]{1,0:T(8,128)}, f32[64,8,256]{2,1,0:T(8,128)}) custom-call(f32[256,128]{1,0:T(8,128)} %get-tuple-element.6.refs_0_, f32[32,128]{1,0:T(8,128)} %get-tuple-element.7.refs_1_, f32[64,8,256]{2,1,0:T(8,128)} %get-tuple-element.8.refs_2_), custom_call_target="tpu_custom_call" | custom-call | tf_op jit(solution)/shard_map/deliver/pallas_call | solution.py:550

commit v4 on v3

--- a/solution.py
+++ b/solution.py
@@ -139,38 +139,42 @@
     last.wait()
 
 
+PACKED = 5
+
+
+def pack(packed, blocks, first=0):
+    side = packed.shape[1]
+    for k, block in enumerate(blocks, first):
+        packed[k * side : (k + 1) * side, :] = block
+
+
+def symmetric_blocks(plain, mixed):
+    side = plain.shape[1] // 2
+    one, two = slice(0, side), slice(side, 2 * side)
+    return [plain[r, c] + mixed[r, c] + mixed[c, r].T for r, c in ((one, one), (one, two), (two, two))]
+
+
 def unfold_sum(whole, terms):
-    half = whole.shape[2]
-    upper = jnp.concatenate([whole[0, half:, :], whole[1, half:, :]], axis=0)
-    first, second = slice(0, half), slice(half, 2 * half)
-    blocks = {
-        (first, first): whole[0, 0:half, :],
-        (second, second): whole[1, 0:half, :],
-        (first, second): upper,
-        (second, first): upper.T,
-    }
-    for (rows, cols), block in blocks.items():
-        terms[0, rows, cols], terms[1, rows, cols], terms[2, rows, cols] = split3(block)
-
-
-def small_inverse_factor(entry):
+    side = whole.shape[2]
+    places = [[(0, 0), (0, 1), (1, 1), (0, 2), (0, 3)], [(2, 2), (2, 3), (3, 3), (1, 2), (1, 3)]]
+    for half in range(2):
+        for k, (i, j) in enumerate(places[half]):
+            block = whole[half, k * side : (k + 1) * side, :]
+            rows, cols = slice(i * side, (i + 1) * side), slice(j * side, (j + 1) * side)
+            terms[0, rows, cols], terms[1, rows, cols], terms[2, rows, cols] = split3(block)
+            if i != j:
+                terms[0, cols, rows], terms[1, cols, rows], terms[2, cols, rows] = split3(block.T)
+
+
+def eliminate(entry):
     n = len(entry)
     entry = [list(row) for row in entry]
     below = [[None] * n for _ in range(n)]
-    result = [[None] * (i + 1) for i in range(n)]
+    pairs = []
     for k in range(0, n, 2):
         a, b, c = entry[k][k], entry[k + 1][k], entry[k + 1][k + 1]
-        det = a * c - b * b
-        inverse = reciprocal(det)
-        over = 1.0 / a
-        ratio = b * over
-        scale_one, scale_two = lax.rsqrt(a), lax.rsqrt(det * over)
-        for j in range(k):
-            result[k][j] = below[k][j] * scale_one
-            result[k + 1][j] = (below[k + 1][j] - ratio * below[k][j]) * scale_two
-        result[k][k] = scale_one
-        result[k + 1][k] = -ratio * scale_two
-        result[k + 1][k + 1] = scale_two
+        inverse = 1.0 / (a * c - b * b)
+        pairs.append((a, b, c, inverse))
         factors = {}
         for i in range(k + 2, n):
             p, q = entry[i][k], entry[i][k + 1]
@@ -182,11 +186,7 @@
             for j in range(k):
                 below[i][j] = below[i][j] - (f * below[k][j] + g * below[k + 1][j])
             below[i][k], below[i][k + 1] = -f, -g
-    return result
-
-
-def reciprocal(value):
-    return 1.0 / value
+    return below, pairs
 
 
 def tree(terms):
@@ -214,16 +214,25 @@
         for k in range(8):
             held[t, k] = lanes_of(tiles[t], first + k)
         held[t, 8] = jnp.where(inside, jnp.where(lane == sub + first, 1.0, 0.0), tiles[t])
-        factor = small_inverse_factor([[row_of(t, j, i) for j in range(i + 1)] for i in range(8)])
+        below, pairs = eliminate([[row_of(t, j, i) for j in range(i + 1)] for i in range(8)])
         spread = [row_of(t, 8, k) for k in range(8)]
-        rows = [tree([factor[i][j] * spread[j] for j in range(i + 1)]) for i in range(8)]
-        value = rows[0]
-        for i in range(1, 8):
-            value = jnp.where(sub == i, rows[i], value)
+        rows = [
+            tree([spread[i]] + [below[i][j] * spread[j] for j in range(i - i % 2)]) for i in range(8)
+        ]
+        value, scaled = None, []
+        for m, (a, b, c, inverse) in enumerate(pairs):
+            p, q = rows[2 * m], rows[2 * m + 1]
+            scaled += [(c * p - b * q) * inverse, (a * q - b * p) * inverse]
+            over = 1.0 / a
+            first_row, second_row = p * lax.rsqrt(a), (q - (b * over) * p) * lax.rsqrt((a * c - b * b) * over)
+            value = first_row if value is None else jnp.where(sub == 2 * m, first_row, value)
+            value = jnp.where(sub == 2 * m + 1, second_row, value)
         found.append(jnp.where(lane < first + 8, value, 0.0))
         if t + 1 == n // 8:
             break
-        solved = [tree([factor[i][k] * rows[i] for i in range(k, 8)]) for k in range(8)]
+        solved = [
+            tree([scaled[k]] + [below[i][k] * scaled[i] for i in range(k - k % 2 + 2, 8)]) for k in range(8)
+        ]
         for u in range(t + 1, n // 8):
             terms = [lanes_of(tiles[u], first + k) * solved[k] for k in range(8)]
             tiles[u] = jnp.where(inside, 0.0, tiles[u]) - tree(terms)
@@ -316,9 +325,10 @@
         cross_sem.at[1],
         {"gx": partner},
     )
-    total[0:rows, :] = gram[0:rows, :] + gram[rows:, :] + gram[rows:, :].T
+    pack(total, symmetric_blocks(gram.at[0:rows, :], gram.at[rows:, :]))
     copy.wait_recv()
-    total[rows:, :] = cross[pl.ds(pl.multiple_of(gx * quarter, 8), quarter), :] + crossed[...]
+    strip = cross[pl.ds(pl.multiple_of(gx * quarter, 8), quarter), :] + crossed[...]
+    pack(total, [strip[:, 0:quarter], strip[:, quarter:]], 3)
     return sends + [copy]
 
 
@@ -384,31 +394,36 @@
         kept_pair[first, at], kept_pair[second, at] = split(value)
 
 
-def gram_two_sums(place, kept_pair, gram, halves, crossed, cross_sem, total):
+def gram_two_sums(place, kept_pair, plain, mixed, halves, crossed, cross_sem, total):
     whole_rows = kept_pair.shape[0] // 2
     half = whole_rows // 2
+    side = half // 2
+    partner = {"gx": place.partner}
     for k in range(2):
         high = kept_pair[half * k : half * (k + 1), :]
-        low = kept_pair[whole_rows + half * k : whole_rows + half * (k + 1), :]
-        gram[...] = dot_nt(low, high)
-        halves[k, 0:half, :] = dot_nt(high, high)
-        halves[k, 0:half, :] += gram[...] + gram[...].T
+        mixed[...] = dot_nt(kept_pair[whole_rows + half * k : whole_rows + half * (k + 1), :], high)
+        plain[...] = dot_nt(high, high)
+        pack(halves.at[k], symmetric_blocks(plain, mixed))
+    head, tail = slice(0, 3 * side), slice(3 * side, 5 * side)
+    copies = [remote(halves.at[place.partner, head, :], crossed.at[head, :], cross_sem.at[0, 0], cross_sem.at[1, 0], partner)]
     high, low = kept_pair[0:half, :], kept_pair[whole_rows : whole_rows + half, :]
-    gram[...] = dot_nt(high, kept_pair[half:whole_rows, :])
-    gram[...] += dot_nt(low, kept_pair[half:whole_rows, :])
-    gram[...] += dot_nt(high, kept_pair[whole_rows + half :, :])
-    halves[0, half:, :] = gram[: half // 2, :]
-    halves[1, half:, :] = gram[half // 2 :, :]
-    copy = remote(halves.at[place.partner], crossed, cross_sem.at[0], cross_sem.at[1], {"gx": place.partner})
-    copy.wait_recv()
-    total[...] = halves[place.gx] + crossed[...]
-    return copy
+    plain[...] = dot_nt(high, kept_pair[half:whole_rows, :])
+    plain[...] += dot_nt(low, kept_pair[half:whole_rows, :])
+    plain[...] += dot_nt(high, kept_pair[whole_rows + half :, :])
+    for k in range(2):
+        rows = slice(k * side, (k + 1) * side)
+        pack(halves.at[k], [plain[rows, 0:side], plain[rows, side:]], 3)
+    copies.append(remote(halves.at[place.partner, tail, :], crossed.at[tail, :], cross_sem.at[0, 1], cross_sem.at[1, 1], partner))
+    for copy, at in zip(copies, (head, tail)):
+        copy.wait_recv()
+        total[at, :] = halves[place.gx, at, :] + crossed[at, :]
+    return copies
 
 
 def kernel(
     plane, field, start_one, start_two, own_one, own_two, core, own, other, pair, pair_p, gram_pair, cross, crossed,
-    terms, basis, start, turned, held, partial, arrived, projected, kept, kept_pair, square, halves, crossed_two, core_parts, landed,
-    load_sem, field_sem, cross_sem, pair_sem, trade_sem, core_sem, *sums
+    terms, basis, start, turned, held, partial, arrived, projected, kept, kept_pair, plain, mixed, halves, crossed_two, core_parts, landed,
+    load_sem, field_sem, cross_sem, cross_two_sem, pair_sem, trade_sem, core_sem, *sums
 ):
     place = Place(plane)
     gx, gy = place.gx, place.gy
@@ -418,7 +433,7 @@
     start[1] = start_two[...].T
     sums_one, sums_two = sums[: len(sums) // 2], sums[len(sums) // 2 :]
     sent = gram_one_sums(
-        place, field, own, other, pair, pair_p, gram_pair, cross, crossed, load_sem, field_sem, cross_sem.at[0], sums_one[0]
+        place, field, own, other, pair, pair_p, gram_pair, cross, crossed, load_sem, field_sem, cross_sem, sums_one[0]
     )
     sum_over_chips(place, *sums_one)
     unfold_sum(sums_one[3], terms)
@@ -434,7 +449,7 @@
         for q in range(len(local)):
             trades[q, d].wait_recv()
         spread_kept(place, kept, kept_pair, place.plane_source(d), cols)
-    sent.append(gram_two_sums(place, kept_pair, square, halves, crossed_two, cross_sem.at[1], sums_two[0]))
+    sent += gram_two_sums(place, kept_pair, plain, mixed, halves, crossed_two, cross_two_sem, sums_two[0])
     sum_over_chips(place, *sums_two)
     unfold_sum(sums_two[3], terms)
     basis[...] = orthonormal(terms, start[1], held)
@@ -445,8 +460,8 @@
     both = jnp.concatenate([basis_high, basis_low], axis=0)
     order = place.plane_order()
     last = []
-    for q in range(2):
-        ranks = part_ranks // 2
+    for q in range(CORE_PARTS):
+        ranks = part_ranks // CORE_PARTS
         at = slice(q * ranks * part_depth, (q + 1) * ranks * part_depth)
         first = dot_nn(both, kept_pair[0:whole_rows, at])
         first = first[:RANK] + first[RANK:] + dot_nn(basis_high, kept_pair[whole_rows:, at])
@@ -471,7 +486,7 @@
     own_two[...] = turned[pl.ds(pl.multiple_of(gy * cols, 8), cols), :]
     for copy in sent + pairs + list(trades.values()):
         copy.wait_send()
-    for copy in local[-2:]:
+    for copy in local[-CORE_PARTS:]:
         copy.wait()
     for copy in last:
         copy.wait_recv()
@@ -486,8 +501,11 @@
         refs[count + k][...] = refs[k][...]
 
 
+CORE_PARTS = 1
+
+
 def parts_of(cols):
-    return [cols // 8, cols // 8, cols // 4, cols // 2]
+    return [cols // 4, cols * 3 // 4]
 
 
 def body(plane, field, start_one, start_two):
@@ -531,18 +549,20 @@
             pltpu.VMEM((whole_rows, part_ranks, 128), f32),
             pltpu.VMEM((2 * whole_rows, part_ranks * 128), bf16),
             pltpu.VMEM((half, half), f32),
-            pltpu.VMEM((2, half * 3 // 2, half), f32),
-            pltpu.VMEM((half * 3 // 2, half), f32),
+            pltpu.VMEM((half, half), f32),
+            pltpu.VMEM((2, PACKED * half // 2, half // 2), f32),
+            pltpu.VMEM((PACKED * half // 2, half // 2), f32),
             pltpu.VMEM((part_ranks, RANK, 128), f32),
             pltpu.VMEM(core_shape, f32),
             dma((cols,)),
             dma((2, cols // 2)),
+            dma((2,)),
             dma((2, 2)),
             dma((2, parts)),
             dma((2, parts, planes)),
-            dma((2, 2, planes)),
-            *sum_scratch(plane, rows * 3 // 2, rows),
-            *sum_scratch(plane, half * 3 // 2, half),
+            dma((2, CORE_PARTS, planes)),
+            *sum_scratch(plane, PACKED * rows // 2, rows // 2),
+            *sum_scratch(plane, PACKED * half // 2, half // 2),
         ],
         compiler_params=pltpu.CompilerParams(collective_id=0, has_side_effects=True, vmem_limit_bytes=VMEM_LIMIT),
         name="hosvd",

time: 120 us -> 117 us (0.975)
  Pallas kernels: 119 us -> 117 us
    pallas_call x1, Pallas kernels: 117 us -> 115 us  [body(): pl.pallas_call(functools.partial(kernel, plane), out_shape=(jax.ShapeDtyp...]
where the time goes in v4:
time: 117 us
  Pallas kernels  117 us (100%)
    pallas_call x1, Pallas kernels, body(): pl.pallas_call(functools.partial(kernel, plane), out_shape=(jax.ShapeDtyp...  115 us

profile of v4, /device:TPU:1, one launch (start us, length us, event | category | flops | bytes accessed | tf_op | source)
XLA Modules:
  0.0 117.2 jit_solution(2445110963138382447)
XLA Ops:
  0.6 114.5 %hosvd.1 = (f32[256,128]{1,0:T(8,128)}, f32[32,128]{1,0:T(8,128)}, f32[64,8,256]{2,1,0:T(8,128)}) custom-call(f32[256,32,256]{2,1,0:T(8,128)} %field.1, f32[512,128]{1,0:T(8,128)} %start_one.1, f32[512,128]{1,0:T(8,128)} %start_two.1), custom_call_target="tpu_custom_call" | custom-call | tf_op jit(solution)/shard_map/hosvd/pallas_call | solution.py:524
  115.2 2.0 %deliver.1 = (f32[256,128]{1,0:T(8,128)}, f32[32,128]{1,0:T(8,128)}, f32[64,8,256]{2,1,0:T(8,128)}) custom-call(f32[256,128]{1,0:T(8,128)} %get-tuple-element.6.refs_0_, f32[32,128]{1,0:T(8,128)} %get-tuple-element.7.refs_1_, f32[64,8,256]{2,1,0:T(8,128)} %get-tuple-element.8.refs_2_), custom_call_target="tpu_custom_call" | custom-call | tf_op jit(solution)/shard_map/deliver/pallas_call | solution.py:570

commit v5 on v4

--- a/solution.py
+++ b/solution.py
@@ -102,7 +102,7 @@
     ]
 
 
-def sum_over_chips(place, total, parts, zparts, whole, rs_sem, z_sem, ag_sem, x_sem):
+def sum_over_chips(place, total, parts, zparts, whole, rs_sem, z_sem, ag_sem, x_sem, meanwhile=None):
     chunk = total.shape[0] // place.np
     order = place.plane_order()
     sent = []
@@ -110,6 +110,8 @@
         peer = place.plane_peer(d)
         piece = total.at[pl.ds(pl.multiple_of(peer * chunk, 8), chunk), :]
         sent.append(remote(piece, parts.at[d], rs_sem.at[0, d], rs_sem.at[1, d], {"gy": peer}))
+    if meanwhile:
+        meanwhile()
     own = pl.ds(pl.multiple_of(place.gy * chunk, 8), chunk)
     value = total[own, :]
     for d, copy in list(zip(order, sent))[::-1]:
@@ -307,8 +309,9 @@
                     )
                 )
     cross[...] = jnp.zeros_like(cross)
-    for c in range(half // 8):
-        for j in range(8 * c, 8 * c + 8):
+    step = 4 * depth
+    for c in range(half // 4):
+        for j in range(4 * c, 4 * c + 4):
             sends[j].wait_recv()
             split_block(other[j], slice(j * depth, (j + 1) * depth), pair_p)
         at = slice(c * step, (c + 1) * step)
@@ -383,14 +386,14 @@
     return pairs, trades, local
 
 
-def spread_kept(place, kept, kept_pair, peer, cols):
+def spread_kept(kept, kept_pair, start, count):
     whole_rows, part_ranks, lanes = kept.shape
     flat = kept.reshape(whole_rows * part_ranks, lanes)
     for r in range(part_ranks):
-        value = flat[pl.ds(peer * cols * part_ranks + r, cols, stride=part_ranks), :]
+        value = flat[pl.ds(start * part_ranks + r, count, stride=part_ranks), :]
         at = slice(r * lanes, (r + 1) * lanes)
-        first = pl.ds(pl.multiple_of(peer * cols, 16), cols)
-        second = pl.ds(pl.multiple_of(whole_rows + peer * cols, 16), cols)
+        first = pl.ds(pl.multiple_of(start, 16), count)
+        second = pl.ds(pl.multiple_of(whole_rows + start, 16), count)
         kept_pair[first, at], kept_pair[second, at] = split(value)
 
 
@@ -422,40 +425,52 @@
 
 def kernel(
     plane, field, start_one, start_two, own_one, own_two, core, own, other, pair, pair_p, gram_pair, cross, crossed,
-    terms, basis, start, turned, held, partial, arrived, projected, kept, kept_pair, plain, mixed, halves, crossed_two, core_parts, landed,
-    load_sem, field_sem, cross_sem, cross_two_sem, pair_sem, trade_sem, core_sem, *sums
+    terms, basis, raw, start, rows_one, turned, held, partial, arrived, projected, kept, kept_pair, plain, mixed, halves, crossed_two, core_parts, landed,
+    load_sem, start_sem, field_sem, cross_sem, cross_two_sem, pair_sem, trade_sem, core_sem, out_sem, *sums
 ):
     place = Place(plane)
     gx, gy = place.gx, place.gy
     rows, cols, depth = field.shape
     place.greet()
-    start[0] = start_one[...].T
-    start[1] = start_two[...].T
+    start_loads = [
+        pltpu.make_async_copy(given, raw.at[k], start_sem.at[k]) for k, given in enumerate((start_one, start_two))
+    ]
+    for copy in start_loads:
+        copy.start()
+
+    def turn_starts():
+        for k, copy in enumerate(start_loads):
+            copy.wait()
+            start[k] = raw[k].T
+
     sums_one, sums_two = sums[: len(sums) // 2], sums[len(sums) // 2 :]
     sent = gram_one_sums(
         place, field, own, other, pair, pair_p, gram_pair, cross, crossed, load_sem, field_sem, cross_sem, sums_one[0]
     )
-    sum_over_chips(place, *sums_one)
+    sum_over_chips(place, *sums_one, meanwhile=turn_starts)
     unfold_sum(sums_one[3], terms)
     basis[...] = orthonormal(terms, start[0], held)
     pairs, trades, local = project(
         place, pair, basis, partial, arrived, projected, kept, pair_sem, trade_sem, cols, depth
     )
-    own_one[...] = basis[:, pl.ds(pl.multiple_of(gx * rows, 128), rows)].T
+    rows_one[...] = basis[:, pl.ds(pl.multiple_of(gx * rows, 128), rows)].T
+    outs = [pltpu.make_async_copy(rows_one, own_one, out_sem.at[0])]
+    outs[0].start()
     for copy in local:
         copy.wait()
-    spread_kept(place, kept, kept_pair, gy, cols)
-    for d in place.plane_order():
-        for q in range(len(local)):
-            trades[q, d].wait_recv()
-        spread_kept(place, kept, kept_pair, place.plane_source(d), cols)
+    spread_kept(kept, kept_pair, gy * cols, cols)
+    for k, some in enumerate(((0, 1), (2,))):
+        for d in place.plane_order():
+            for q in some:
+                trades[q, d].wait_recv()
+            spread_kept(kept, kept_pair, place.plane_source(d) * cols + k * (cols // 2), cols // 2)
     sent += gram_two_sums(place, kept_pair, plain, mixed, halves, crossed_two, cross_two_sem, sums_two[0])
     sum_over_chips(place, *sums_two)
     unfold_sum(sums_two[3], terms)
     basis[...] = orthonormal(terms, start[1], held)
     whole_rows, part_ranks, part_depth = kept.shape
     splits = depth // part_depth
-    each = core.shape[1]
+    each = landed.shape[1]
     basis_high, basis_low = split(basis[...])
     both = jnp.concatenate([basis_high, basis_low], axis=0)
     order = place.plane_order()
@@ -483,16 +498,20 @@
         stays.start()
         local.append(stays)
     turned[...] = basis[...].T
-    own_two[...] = turned[pl.ds(pl.multiple_of(gy * cols, 8), cols), :]
+    outs.append(pltpu.make_async_copy(turned.at[pl.ds(pl.multiple_of(gy * cols, 8), cols), :], own_two, out_sem.at[1]))
+    outs[1].start()
     for copy in sent + pairs + list(trades.values()):
         copy.wait_send()
     for copy in local[-CORE_PARTS:]:
         copy.wait()
     for copy in last:
         copy.wait_recv()
-    core[...] = landed[...]
+    outs.append(pltpu.make_async_copy(landed, core, out_sem.at[2]))
+    outs[2].start()
     for copy in last:
         copy.wait_send()
+    for copy in outs:
+        copy.wait()
 
 
 def deliver(*refs):
@@ -505,7 +524,7 @@
 
 
 def parts_of(cols):
-    return [cols // 4, cols * 3 // 4]
+    return [cols // 4, cols // 4, cols // 2]
 
 
 def body(plane, field, start_one, start_two):
@@ -519,6 +538,7 @@
     parts = len(parts_of(cols))
     dma = pltpu.SemaphoreType.DMA
     vmem = pl.BlockSpec(memory_space=pltpu.VMEM)
+    anywhere = pl.BlockSpec(memory_space=pl.ANY)
     core_shape = (RANK // 2, RANK // planes, depth)
     size = max(2 * rows, whole_rows)
     outs = pl.pallas_call(
@@ -528,8 +548,8 @@
             jax.ShapeDtypeStruct((cols, RANK), f32),
             jax.ShapeDtypeStruct(core_shape, f32),
         ),
-        in_specs=[pl.BlockSpec(memory_space=pl.ANY), vmem, vmem],
-        out_specs=(vmem, vmem, vmem),
+        in_specs=[anywhere, anywhere, anywhere],
+        out_specs=(anywhere, anywhere, anywhere),
         scratch_shapes=[
             pltpu.VMEM((cols, rows, depth), f32),
             pltpu.VMEM((cols // 2, rows, depth), f32),
@@ -540,7 +560,9 @@
             pltpu.VMEM((rows // 2, rows), f32),
             pltpu.VMEM((3, size, size), bf16),
             pltpu.VMEM((RANK, size), f32),
+            pltpu.VMEM((2, size, RANK), f32),
             pltpu.VMEM((2, RANK, size), f32),
+            pltpu.VMEM((rows, RANK), f32),
             pltpu.VMEM((size, RANK), f32),
             pltpu.VMEM((RANK // 8, 9, 8, RANK), f32),
             pltpu.VMEM((cols, RANK, depth), f32),
@@ -555,12 +577,14 @@
             pltpu.VMEM((part_ranks, RANK, 128), f32),
             pltpu.VMEM(core_shape, f32),
             dma((cols,)),
+            dma((2,)),
             dma((2, cols // 2)),
             dma((2,)),
             dma((2, 2)),
             dma((2, parts)),
             dma((2, parts, planes)),
             dma((2, CORE_PARTS, planes)),
+            dma((3,)),
             *sum_scratch(plane, PACKED * rows // 2, rows // 2),
             *sum_scratch(plane, PACKED * half // 2, half // 2),
         ],

time: 117 us -> 116 us (level)
  Pallas kernels: 117 us -> 115 us
where the time goes in v5:
time: 116 us
  Pallas kernels  115 us (99%)
    pallas_call x1, Pallas kernels, body(): pl.pallas_call(functools.partial(kernel, plane), out_shape=(jax.ShapeDtyp...  113 us

profile of v5, /device:TPU:1, one launch (start us, length us, event | category | flops | bytes accessed | tf_op | source)
XLA Modules:
  0.0 116.1 jit_solution(15092857878943214404)
XLA Ops:
  0.6 113.5 %hosvd.1 = (f32[256,128]{1,0:T(8,128)}, f32[32,128]{1,0:T(8,128)}, f32[64,8,256]{2,1,0:T(8,128)}) custom-call(f32[256,32,256]{2,1,0:T(8,128)} %field.1, f32[512,128]{1,0:T(8,128)} %start_one.1, f32[512,128]{1,0:T(8,128)} %start_two.1), custom_call_target="tpu_custom_call" | custom-call | tf_op jit(solution)/shard_map/hosvd/pallas_call | solution.py:544
  114.1 2.0 %deliver.1 = (f32[256,128]{1,0:T(8,128)}, f32[32,128]{1,0:T(8,128)}, f32[64,8,256]{2,1,0:T(8,128)}) custom-call(f32[256,128]{1,0:T(8,128)} %get-tuple-element.6.refs_0_, f32[32,128]{1,0:T(8,128)} %get-tuple-element.7.refs_1_, f32[64,8,256]{2,1,0:T(8,128)} %get-tuple-element.8.refs_2_), custom_call_target="tpu_custom_call" | custom-call | tf_op jit(solution)/shard_map/deliver/pallas_call | solution.py:594
